TPU v7x, 32 devices: a whole 2x2x4 slice. The times are simulated.
32 devices in a mesh: pool: 8 (over y, x, core), tp: 4 (over z).
Axes of the slice: x: 2, y: 2, z: 4, core: 2. Of those that a mesh axis runs over, the one named last changes fastest.
Arguments:
- turn_query: bfloat16 [4096, 2048], P('pool', 'tp'), may hold values from -16 to 16
- turn_key: bfloat16 [4096, 512], P('pool', 'tp'), may hold values from -16 to 16, as said below
- turn_value: bfloat16 [4096, 512], P('pool', 'tp'), may hold values from -6 to 6
- pool_keys: bfloat16 [512, 128, 512], P('pool', None, 'tp'), may hold values from -16 to 16, as said below
- pool_values: bfloat16 [512, 128, 512], P('pool', None, 'tp'), may hold values from -6 to 6
- seat_session: int32 [16], replicated, may hold values from 0 to 15, as said below
- history_len: int32 [16], replicated, may hold values from 1 to 4096, as said below
- block_map: int32 [16, 32], replicated, may hold values from 0 to 511, as said below
- out_weight: bfloat16 [2048, 8192], P('tp', 'pool'), may hold values from -0.1875 to 0.1875
Outputs:
- layer_out: bfloat16 [4096, 8192], P('pool', 'tp')
Inputs may be any that keep to these rules, and one draw needn't show every extreme that they name: `seat_session`: A permutation of the sessions. `history_len`: the sessions of one owner, chosen afresh in every draw, have length 4096. Every slot of the pool is named exactly once. Call block j of session s live when j * 128 < history_len[s]; the slot's pool index is block_map[s, j] // 64. The live blocks of one pool index that belong to the sessions of one owner number at most 8; some owner receives exactly 8 from every pool index. `turn_key`: Real-valued keys. `pool_keys`: Real-valued keys; slots not named by a live block hold values that are never read.
All inputs are finite; a program needn't handle non-finite values.
Results may differ from a plain program's by a relative error of at most 0.019.
Values may be sent and summed in bfloat16 or wider, within the bound.
A program may use at most 128 MiB of HBM per device.

v0:
```python
import functools
import math

import jax
import jax.numpy as jnp
import numpy as np
from jax import lax
from jax.experimental import pallas as pl
from jax.experimental.pallas import tpu as pltpu
from jax.sharding import PartitionSpec as P

rope_base = 1000000.0
MESH = pl.DeviceIdType.MESH
F32 = jnp.float32
BF16 = jnp.bfloat16
dot = functools.partial(jnp.dot, preferred_element_type=F32)


def kernel(
    pools,
    tps,
    seats,
    cap,
    meta_ref,
    tq_ref,
    tk_ref,
    tv_ref,
    cos_far,
    sin_far,
    cos_near,
    sin_near,
    pool_k,
    pool_v,
    weight,
    out_ref,
    send_k,
    send_v,
    keys,
    vals,
    gathered,
    attended,
    queries,
    wide_keys,
    scores,
    probs,
    flipped,
    acc,
    top,
    total,
    k_send,
    k_recv,
    v_send,
    v_recv,
    s_send,
    s_recv,
    g_send,
    g_recv,
    f_send,
    a_send,
    a_recv,
    local_sem,
):
    me = lax.axis_index("pool")
    row = lax.axis_index("tp")
    block = pool_k.shape[1]
    head = pool_k.shape[2]
    turn = tq_ref.shape[0] // seats
    group = tq_ref.shape[1] // head
    wide = group * turn
    chips = pools // 2
    share = pools // tps
    part = weight.shape[0] // pools
    w_cols = weight.shape[1]
    sibling = me + 1 - 2 * lax.rem(me, 2)
    core = lax.rem(me, 2)
    chip = me // 2
    target_row = me // share
    at_home = target_row == row

    barrier = pltpu.get_barrier_semaphore()

    def greet(pool_index, tp_index):
        pl.semaphore_signal(barrier, inc=1, device_id=(pool_index, tp_index), device_id_type=MESH)

    def greet_pool(i, carry):
        greet(lax.rem(me + i, pools), row)
        return carry

    lax.fori_loop(1, pools, greet_pool, 0)

    @pl.when(row > 0)
    def _():
        greet(me, row - 1)

    @pl.when(row < tps - 1)
    def _():
        greet(me, row + 1)

    def greet_source(i, carry):
        source_pool = row * share + i // tps
        source_row = lax.rem(i, tps)

        @pl.when(jnp.logical_not((source_pool == me) & (source_row == row)))
        def _():
            greet(source_pool, source_row)

        return carry

    lax.fori_loop(0, share * tps, greet_source, 0)
    greeted = (
        2 * pools
        - 1
        - at_home.astype(jnp.int32)
        + (row > 0).astype(jnp.int32)
        + (row < tps - 1).astype(jnp.int32)
    )
    pl.semaphore_wait(barrier, greeted)

    def kv_copies(q):
        return (
            pltpu.make_async_remote_copy(
                src_ref=send_k.at[q],
                dst_ref=keys.at[me],
                send_sem=k_send.at[q],
                recv_sem=k_recv.at[me],
                device_id=(q, row),
                device_id_type=MESH,
            ),
            pltpu.make_async_remote_copy(
                src_ref=send_v.at[q],
                dst_ref=vals.at[me],
                send_sem=v_send.at[q],
                recv_sem=v_recv.at[me],
                device_id=(q, row),
                device_id_type=MESH,
            ),
        )

    def kv_arrival(s):
        return (
            pltpu.make_async_remote_copy(
                src_ref=keys.at[s],
                dst_ref=keys.at[s],
                send_sem=k_send.at[s],
                recv_sem=k_recv.at[s],
                device_id=(s, row),
                device_id_type=MESH,
            ),
            pltpu.make_async_remote_copy(
                src_ref=vals.at[s],
                dst_ref=vals.at[s],
                send_sem=v_send.at[s],
                recv_sem=v_recv.at[s],
                device_id=(s, row),
                device_id_type=MESH,
            ),
        )

    def scatter_copy(q):
        return pltpu.make_async_remote_copy(
            src_ref=weight.at[pl.ds(pl.multiple_of(q * part, part), part)],
            dst_ref=gathered.at[
                q,
                row,
                :,
                pl.ds(pl.multiple_of(lax.rem(me, share) * w_cols, w_cols), w_cols),
            ],
            send_sem=s_send.at[q],
            recv_sem=s_recv.at[lax.rem(me, share) * tps + row],
            device_id=(q, target_row),
            device_id_type=MESH,
        )

    own_w = pltpu.make_async_copy(
        weight.at[pl.ds(pl.multiple_of(me * part, part), part)],
        gathered.at[
            me, row, :, pl.ds(pl.multiple_of(lax.rem(me, share) * w_cols, w_cols), w_cols)
        ],
        local_sem.at[0],
    )

    def start_scatter(i, carry):
        q = lax.rem(me + i, pools)
        scatter_copy(q).start()
        return carry

    lax.fori_loop(1, pools, start_scatter, 0)

    @pl.when(at_home)
    def _():
        own_w.start()

    @pl.when(jnp.logical_not(at_home))
    def _():
        scatter_copy(me).start()

    def start_kv(i, carry):
        q = lax.rem(me + i, pools)
        for r in range(cap):
            slot = meta_ref[q, r]
            send_k[q, r] = pool_k[slot]
            send_v[q, r] = pool_v[slot]
        for copy in kv_copies(q):
            copy.start()
        return carry

    lax.fori_loop(1, pools, start_kv, 0)
    for r in range(cap):
        slot = meta_ref[me, r]
        keys[me, r] = pool_k[slot]
        vals[me, r] = pool_v[slot]

    halves = 2
    half_rows = tps // halves

    def slab_copy(slab, half, pool_index, send_sem):
        piece = gathered.at[slab, pl.ds(half * half_rows, half_rows)]
        return pltpu.make_async_remote_copy(
            src_ref=piece,
            dst_ref=piece,
            send_sem=send_sem,
            recv_sem=g_recv.at[slab, half],
            device_id=(pool_index, row),
            device_id_type=MESH,
        )

    def chip_peer(i):
        return lax.rem(chip + i, chips) * 2 + core

    def chip_source(i):
        return lax.rem(chip + chips - i, chips) * 2 + core

    relay = chips == 4
    next_x = (chip + 1 - 2 * lax.rem(chip, 2)) * 2 + core
    next_y = lax.rem(chip + 2, 4) * 2 + core
    across = (lax.rem(chip + 2, 4) + 1 - 2 * lax.rem(chip, 2)) * 2 + core

    def own_slab_sends():
        if relay:
            order = [(next_x, 0), (next_y, 1), (next_x, 1), (next_y, 0)]
            return [(me, half, peer, g_send.at[n]) for n, (peer, half) in enumerate(order)]
        return []

    def relay_sends():
        return [(next_x, 0, next_y, g_send.at[4]), (next_y, 1, next_x, g_send.at[5])]

    def core_send(n, slab, half):
        return (slab, half, sibling, f_send.at[n, half])

    def start_gather():
        def wait_piece(i, carry):
            piece_pool = row * share + i // tps
            piece_row = lax.rem(i, tps)

            @pl.when(jnp.logical_not((piece_pool == me) & (piece_row == row)))
            def _():
                landing = gathered.at[
                    me,
                    piece_row,
                    :,
                    pl.ds(pl.multiple_of((i // tps) * w_cols, w_cols), w_cols),
                ]
                pltpu.make_async_remote_copy(
                    src_ref=landing,
                    dst_ref=landing,
                    send_sem=s_send.at[0],
                    recv_sem=s_recv.at[i],
                    device_id=(piece_pool, piece_row),
                    device_id_type=MESH,
                ).wait_recv()

            return carry

        lax.fori_loop(0, share * tps, wait_piece, 0)

        @pl.when(at_home)
        def _():
            own_w.wait()

        if relay:
            for item in own_slab_sends():
                slab_copy(*item).start()
        else:

            def start_slab(i, carry):
                for half in range(halves):
                    slab_copy(me, half, chip_peer(i), g_send.at[i * halves + half]).start()
                return carry

            lax.fori_loop(1, chips, start_slab, 0)
        for half in range(halves):
            slab_copy(*core_send(0, me, half)).start()

    def pass_on(n, slab, half, onward=None):
        to_core = slab_copy(*core_send(n, slab, half))
        to_core.wait_recv()
        if onward is not None:
            slab_copy(*onward).start()
        to_core.start()

    factor = math.log2(math.e) / math.sqrt(head)
    tables = []
    for e in range(seats):
        far, near = meta_ref[4 * pools + e, 0], meta_ref[4 * pools + e, 1]
        ca, sa = cos_far[pl.ds(far, 1), :], sin_far[pl.ds(far, 1), :]
        cb, sb = cos_near[pl.ds(near, 1), :], sin_near[pl.ds(near, 1), :]
        ca, sa = ca * cb - sa * sb, sa * cb + ca * sb
        cb, sb = cos_near[...], sin_near[...]
        tables.append((ca * cb - sa * sb, sa * cb + ca * sb))

    def rope(x, cosine, sine):
        return x * cosine + pltpu.roll(x, head // 2, 1) * sine

    lanes = lax.broadcasted_iota(jnp.int32, (turn, wide), 1)
    unseen = lax.broadcasted_iota(jnp.int32, (turn, wide), 0) > lax.rem(lanes, turn)
    for e in range(seats):
        cosine, sine = tables[e]
        rows = slice(e * turn, (e + 1) * turn)
        for h in range(group):
            x = tq_ref[rows, h * head : (h + 1) * head].astype(F32)
            turned = rope(x, cosine, sine) * factor
            queries[e * head : (e + 1) * head, h * turn : (h + 1) * turn] = turned.T.astype(BF16)
        new_keys = rope(tk_ref[rows, :].astype(F32), cosine, sine).astype(BF16)
        s = jnp.where(unseen, -jnp.inf, dot(new_keys, queries[e * head : (e + 1) * head, :]))
        best = jnp.max(s, axis=0, keepdims=True)
        p = jnp.exp2(s - best)
        top[e : e + 1, :] = best
        total[e : e + 1, :] = jnp.sum(p, axis=0, keepdims=True)
        flipped_new = tv_ref[rows, :].astype(F32).T.astype(BF16)
        acc[e * head : (e + 1) * head, :] = dot(flipped_new, p.astype(BF16))

    depth = lax.broadcasted_iota(jnp.int32, (block, 1), 0)

    def attend(source):
        tops = [top[e : e + 1, :] for e in range(seats)]
        owners = []
        for b in range(cap):
            far, seat = meta_ref[pools + source, b], meta_ref[2 * pools + source, b]
            owners.append(seat)
            ca, sa = cos_far[pl.ds(far, 1), :], sin_far[pl.ds(far, 1), :]
            cb, sb = cos_near[0:block, :], sin_near[0:block, :]
            x = keys[source, b].astype(F32)
            turned = rope(x, ca * cb - sa * sb, sa * cb + ca * sb)
            upright = vals[source, b].astype(F32).T
            span = slice(b * block, (b + 1) * block)
            for e in range(seats):
                part_e = slice(e * head, (e + 1) * head)
                wide_keys[span, part_e] = jnp.where(seat == e, turned, 0.0).astype(BF16)
                flipped[part_e, span] = jnp.where(seat == e, upright, 0.0).astype(BF16)
        run = math.gcd(cap, 4)
        for first in range(0, cap, run):
            several = dot(
                wide_keys[first * block : (first + run) * block, :], queries[...]
            )
            for b in range(first, first + run):
                s = several[(b - first) * block : (b - first + 1) * block, :]
                s = jnp.where(depth < meta_ref[3 * pools + source, b], s, -jnp.inf)
                scores[b * block : (b + 1) * block, :] = s
                best = jnp.max(s, axis=0, keepdims=True)
                for e in range(seats):
                    tops[e] = jnp.maximum(tops[e], jnp.where(owners[b] == e, best, -jnp.inf))
        alphas = [jnp.exp2(top[e : e + 1, :] - tops[e]) for e in range(seats)]
        sums = [total[e : e + 1, :] * alphas[e] for e in range(seats)]
        for b in range(cap):
            span = slice(b * block, (b + 1) * block)
            base = tops[0]
            for e in range(1, seats):
                base = jnp.where(owners[b] == e, tops[e], base)
            p = jnp.exp2(scores[span, :] - base)
            added = jnp.sum(p, axis=0, keepdims=True)
            for e in range(seats):
                sums[e] = sums[e] + jnp.where(owners[b] == e, added, 0.0)
            probs[span, :] = p.astype(BF16)
        gained = dot(flipped[...], probs[...])
        for e in range(seats):
            rows = slice(e * head, (e + 1) * head)
            acc[rows, :] = acc[rows, :] * alphas[e] + gained[rows, :]
            top[e : e + 1, :] = tops[e]
            total[e : e + 1, :] = sums[e]

    def step(i, carry):
        source = lax.rem(me + pools - i, pools)

        @pl.when(i > 0)
        def _():
            for copy in kv_arrival(source):
                copy.wait_recv()

        @pl.when(i == pools - 3)
        def _():
            start_gather()

        attend(source)
        return carry

    lax.fori_loop(0, pools, step, 0)

    for e in range(seats):
        rows = slice(e * turn, (e + 1) * turn)
        final = acc[e * head : (e + 1) * head, :] / total[e : e + 1, :]
        for h in range(group):
            attended[row, rows, h * head : (h + 1) * head] = (
                final[:, h * turn : (h + 1) * turn].T.astype(BF16)
            )

    def slot_copy(slot, neighbour, way, hop):
        return pltpu.make_async_remote_copy(
            src_ref=attended.at[slot],
            dst_ref=attended.at[slot],
            send_sem=a_send.at[way, hop],
            recv_sem=a_recv.at[slot],
            device_id=(me, neighbour),
            device_id_type=MESH,
        )

    def hop_sends(hop, act):
        @pl.when((row - hop >= 0) & (row < tps - 1))
        def _():
            act(slot_copy(row - hop, row + 1, 0, hop))

        @pl.when((row + hop < tps) & (row > 0))
        def _():
            act(slot_copy(row + hop, row - 1, 1, hop))

    def hop_waits(hop):
        @pl.when(row - hop >= 0)
        def _():
            slot_copy(row - hop, row - 1, 0, 0).wait_recv()

        @pl.when(row + hop < tps)
        def _():
            slot_copy(row + hop, row + 1, 1, 0).wait_recv()

    hop_sends(0, lambda copy: copy.start())
    if relay:
        first, second = relay_sends()
        passes = [
            [(1, next_x, 0, first), (2, next_y, 1, second)],
            [(1, next_x, 1), (2, next_y, 0)],
            [(3, across, 0), (3, across, 1)],
        ]
    else:
        passes = []
    for hop in range(1, tps):
        if passes:
            for item in passes.pop(0):
                pass_on(*item)
        hop_waits(hop)
        if hop < tps - 1:
            hop_sends(hop, lambda copy: copy.start())
    for group_of in passes:
        for item in group_of:
            pass_on(*item)
    if not relay:

        def rest(i, carry):
            for half in range(halves):
                pass_on(i, chip_source(i), half)
            return carry

        lax.fori_loop(1, chips, rest, 0)

    def wait_passed(i, carry):
        slab = chip_source(i) - core + lax.rem(sibling, 2)
        for half in range(halves):
            slab_copy(slab, half, sibling, g_send.at[0]).wait_recv()
        return carry

    lax.fori_loop(0, chips, wait_passed, 0)

    tile = 256

    def project(n, carry):
        cols = pl.ds(pl.multiple_of(n * tile, tile), tile)
        result = jnp.zeros((out_ref.shape[0], tile), F32)
        for t in range(tps):
            w = gathered[:, t, :, cols].reshape(pools * part, tile)
            result = result + dot(attended[t], w)
        out_ref[:, cols] = result.astype(BF16)
        return carry

    lax.fori_loop(0, out_ref.shape[1] // tile, project, 0)

    def wait_sends(i, carry):
        q = lax.rem(me + i, pools)
        for copy in kv_copies(q):
            copy.wait_send()
        scatter_copy(q).wait_send()
        return carry

    lax.fori_loop(1, pools, wait_sends, 0)

    @pl.when(jnp.logical_not(at_home))
    def _():
        scatter_copy(me).wait_send()

    if relay:
        for item in own_slab_sends() + relay_sends():
            slab_copy(*item).wait_send()
        for n, slab in enumerate((me, next_x, next_y, across)):
            for half in range(halves):
                slab_copy(*core_send(n, slab, half)).wait_send()
    else:

        def wait_slabs(i, carry):
            for half in range(halves):
                slab_copy(me, half, chip_peer(i), g_send.at[i * halves + half]).wait_send()
                slab_copy(*core_send(i, chip_source(i), half)).wait_send()
            return carry

        lax.fori_loop(1, chips, wait_slabs, 0)
        for half in range(halves):
            slab_copy(*core_send(0, me, half)).wait_send()
    for hop in range(tps - 1):
        hop_sends(hop, lambda copy: copy.wait_send())


def plan(pools, seats, cap, blocks_here, block, seat_ref, len_ref, map_ref, out_ref):
    me = lax.axis_index("pool")
    slots, block_count = map_ref.shape[0], map_ref.shape[1]
    seated = pools * seats

    def iota(shape, dim):
        return lax.broadcasted_iota(jnp.int32, shape, dim)

    def lane_sum(mask, x):
        return jnp.sum(jnp.where(mask, x, 0.0), axis=1, keepdims=True)

    sits = seat_ref[...] == iota((seated, slots), 1)
    lengths = lane_sum(sits, len_ref[...].astype(F32))
    all_slots = map_ref[...].astype(F32)
    seat_map = jnp.zeros((seated, block_count), F32)
    for session in range(slots):
        seat_map = seat_map + jnp.where(
            seat_ref[...] == session, all_slots[session : session + 1, :], 0.0
        )
    home = jnp.floor(seat_map * (1.0 / blocks_here))
    slot = seat_map - home * blocks_here
    numbers = iota((seated, block_count), 1).astype(F32)
    alive = numbers * block < lengths
    upto = jnp.where(
        iota((block_count, block_count), 0) <= iota((block_count, block_count), 1), 1.0, 0.0
    )

    leaving = alive & (home == me.astype(F32))
    flags = jnp.where(leaving, 1.0, 0.0)
    row_a, row_b = iota((seated, seated), 0), iota((seated, seated), 1)
    before = jnp.where((row_b < row_a) & (row_b // seats == row_a // seats), 1.0, 0.0)
    offset = jnp.sum(dot(before, flags), axis=1, keepdims=True)
    rank = dot(flags, upto) - 1.0 + offset
    merge = jnp.where(
        iota((pools, seated), 0) == iota((pools, seated), 1) // seats, 1.0, 0.0
    )
    for r in range(cap):
        picked = dot(merge, jnp.where(leaving & (rank == r), slot, 0.0))
        out_ref[0:pools, r : r + 1] = jnp.sum(picked, axis=1, keepdims=True).astype(jnp.int32)

    sources = iota((pools, block_count), 0).astype(F32)
    order = iota((pools, block_count), 1).astype(F32)
    taken = jnp.zeros((pools, 1), F32)
    found = [[jnp.zeros((pools, 1), F32) for r in range(cap)] for kind in range(3)]
    rows = iota((seated, block_count), 0)
    for e in range(seats):
        mine = rows == me * seats + e
        own_home = jnp.sum(jnp.where(mine, home, 0.0), axis=0, keepdims=True)
        own_length = jnp.sum(
            jnp.where(mine, lengths + jnp.zeros_like(home), 0.0), axis=0, keepdims=True
        )
        coming = (order * block < own_length) & (own_home == sources)
        flags = jnp.where(coming, 1.0, 0.0)
        rank = dot(flags, upto) - 1.0 + taken
        taken = taken + jnp.sum(flags, axis=1, keepdims=True)
        for r in range(cap):
            hit = coming & (rank == r)
            found[0][r] = found[0][r] + lane_sum(hit, order)
            found[1][r] = found[1][r] + lane_sum(hit, jnp.full_like(order, e + 1.0))
            found[2][r] = found[2][r] + lane_sum(hit, own_length - order * block)
        length = own_length[:, 0:1]
        far = jnp.floor(length * (1.0 / block))
        out_ref[4 * pools + e : 4 * pools + e + 1, 0:1] = far.astype(jnp.int32)
        out_ref[4 * pools + e : 4 * pools + e + 1, 1:2] = (length - far * block).astype(jnp.int32)
    for kind in range(3):
        for r in range(cap):
            value = found[kind][r] - (1.0 if kind == 1 else 0.0)
            out_ref[(kind + 1) * pools : (kind + 2) * pools, r : r + 1] = value.astype(jnp.int32)


def local(
    turn_query,
    turn_key,
    turn_value,
    pool_keys,
    pool_values,
    seat_session,
    history_len,
    block_map,
    out_weight,
):
    pools = lax.axis_size("pool")
    tps = lax.axis_size("tp")
    block, head = pool_keys.shape[1:]
    block_count = block_map.shape[1]
    seats = seat_session.shape[0] // pools
    cap = seats * block_count // pools
    rows, width = turn_query.shape
    turn = rows // seats
    group = width // head
    wide = group * turn
    part = out_weight.shape[0] // pools
    out_cols = out_weight.shape[1] * pools // tps

    in_vmem = pl.BlockSpec(memory_space=pltpu.VMEM)
    in_smem = pl.BlockSpec(memory_space=pltpu.SMEM)
    anywhere = pl.BlockSpec(memory_space=pl.ANY)
    dma = pltpu.SemaphoreType.DMA

    meta = pl.pallas_call(
        functools.partial(plan, pools, seats, cap, pool_keys.shape[0], block),
        out_shape=jax.ShapeDtypeStruct((4 * pools + 8, max(cap, 2)), jnp.int32),
        in_specs=[in_vmem] * 3,
        out_specs=in_vmem,
    )(seat_session[:, None], history_len[None, :], block_map)

    half = head // 2
    inverse = rope_base ** (-2.0 * np.arange(half) / head)
    inverse = np.concatenate([inverse, inverse])
    signs = np.concatenate([-np.ones(half), np.ones(half)])
    near = np.arange(turn)[:, None] * inverse[None, :]
    far = (np.arange(block_count + 1) * block)[:, None] * inverse[None, :]
    cos_near = jnp.asarray(np.cos(near), F32)
    sin_near = jnp.asarray(np.sin(near) * signs, F32)
    cos_far = jnp.asarray(np.cos(far), F32)
    sin_far = jnp.asarray(np.sin(far) * signs, F32)

    chips = pools // 2
    return pl.pallas_call(
        functools.partial(kernel, pools, tps, seats, cap),
        out_shape=jax.ShapeDtypeStruct((rows, out_cols), BF16),
        in_specs=[in_smem] + [in_vmem] * 9 + [anywhere],
        out_specs=in_vmem,
        scratch_shapes=[
            pltpu.VMEM((pools, cap, block, head), BF16),
            pltpu.VMEM((pools, cap, block, head), BF16),
            pltpu.VMEM((pools, cap, block, head), BF16),
            pltpu.VMEM((pools, cap, block, head), BF16),
            pltpu.VMEM((pools, tps, part, out_cols), BF16),
            pltpu.VMEM((tps, rows, width), BF16),
            pltpu.VMEM((seats * head, wide), BF16),
            pltpu.VMEM((cap * block, seats * head), BF16),
            pltpu.VMEM((cap * block, wide), F32),
            pltpu.VMEM((cap * block, wide), BF16),
            pltpu.VMEM((seats * head, cap * block), BF16),
            pltpu.VMEM((seats * head, wide), F32),
            pltpu.VMEM((seats, wide), F32),
            pltpu.VMEM((seats, wide), F32),
            dma((pools,)),
            dma((pools,)),
            dma((pools,)),
            dma((pools,)),
            dma((pools,)),
            dma((pools,)),
            dma((2 * chips,)),
            dma((pools, 2)),
            dma((chips, 2)),
            dma((2, tps)),
            dma((tps,)),
            dma((1,)),
        ],
        compiler_params=pltpu.CompilerParams(
            collective_id=0, has_side_effects=True, vmem_limit_bytes=56 * 1024 * 1024
        ),
    )(
        meta,
        turn_query,
        turn_key,
        turn_value,
        cos_far,
        sin_far,
        cos_near,
        sin_near,
        pool_keys,
        pool_values,
        out_weight,
    )


def solution(mesh):
    return jax.shard_map(
        local,
        mesh=mesh,
        in_specs=(
            P("pool", "tp"),
            P("pool", "tp"),
            P("pool", "tp"),
            P("pool", None, "tp"),
            P("pool", None, "tp"),
            P(),
            P(),
            P(),
            P("tp", "pool"),
        ),
        out_specs=P("pool", "tp"),
        check_vma=False,
    )
```

profile of v0, /device:TPU:0, one launch (start us, length us, event | category | flops | bytes accessed | tf_op | source)
XLA Modules:
  0.0 149.0 jit_solution(18288167002578847781)
XLA Ops:
  0.0 1.3 copy.14.seat_ref
  1.3 1.9 %shard_map.127.meta_ref = s32[40,8]{1,0:T(8,128)} custom-call(s32[16,1]{1,0:T(8,128)} %copy.14.seat_ref, s32[1,16]{1,0:T(1,128)} %bitcast.2, s32[16,32]{1,0:T(8,128)} %map_ref.1), custom_call_target="tpu_custom_call" | custom-call | tf_op jit(solution)/shard_map/pallas_call | solution.py:617
  3.3 142.5 %shard_map.128 = bf16[512,2048]{1,0:T(8,128)(2,1)} custom-call(s32[40,8]{1,0:T(8,128)} %shard_map.127.meta_ref, bf16[512,512]{1,0:T(8,128)(2,1)} %tq_ref.1, bf16[512,128]{1,0:T(8,128)(2,1)} %tk_ref.1, bf16[512,128]{1,0:T(8,128)(2,1)} %tv_ref.1, f32[33,128]{1,0:T(8,128)} %constant.10.clone.cos_far, f32[33,128]{1,0:T(8,128)} %constant.11.clone.sin_far, ...), custom_call_target="tpu_custom_call" | custom-call | tf_op jit(solution)/shard_map/pallas_call | solution.py:636
  145.8 3.2 %copy.16 = bf16[512,2048]{1,0:T(8,128)(2,1)} copy(bf16[512,2048]{1,0:T(8,128)(2,1)} %shard_map.128) | data formatting | bytes 4194304
where the time goes:
time: 149 us
  Pallas kernels  144 us (97%)
  local copies, waits for them, and re-layouts  4.48 us (3%)
    pallas_call x1, Pallas kernels, local(): pl.pallas_call(functools.partial(kernel, pools, tps, seats, cap), out_sha...  143 us
    unnamed x1, local copies, waits for them, and re-layouts  3.16 us

commit v1 on v0

--- a/solution.py
+++ b/solution.py
@@ -47,6 +47,7 @@
     acc,
     top,
     total,
+    partial,
     k_send,
     k_recv,
     v_send,
@@ -386,7 +387,7 @@
             for copy in kv_arrival(source):
                 copy.wait_recv()
 
-        @pl.when(i == pools - 3)
+        @pl.when(i == pools - 1)
         def _():
             start_gather()
 
@@ -460,26 +461,57 @@
 
         lax.fori_loop(1, chips, rest, 0)
 
-    def wait_passed(i, carry):
-        slab = chip_source(i) - core + lax.rem(sibling, 2)
+    def wait_slab(slab):
         for half in range(halves):
             slab_copy(slab, half, sibling, g_send.at[0]).wait_recv()
-        return carry
-
-    lax.fori_loop(0, chips, wait_passed, 0)
-
-    tile = 256
-
-    def project(n, carry):
-        cols = pl.ds(pl.multiple_of(n * tile, tile), tile)
-        result = jnp.zeros((out_ref.shape[0], tile), F32)
-        for t in range(tps):
-            w = gathered[:, t, :, cols].reshape(pools * part, tile)
-            result = result + dot(attended[t], w)
-        out_ref[:, cols] = result.astype(BF16)
-        return carry
-
-    lax.fori_loop(0, out_ref.shape[1] // tile, project, 0)
+
+    tile = 512
+    tiles = out_ref.shape[1] // tile
+    out_rows = out_ref.shape[0]
+    if relay and 2 * part == head:
+        for n, slab in enumerate((me, next_x, next_y, across)):
+            wait_slab(slab + sibling - me)
+            pair = slab // 2
+            spans = pl.ds(pl.multiple_of(pair * head, head), head)
+            left = jnp.concatenate([attended[t, :, spans] for t in range(tps)], axis=1)
+
+            def project(c, carry, n=n, pair=pair, left=left):
+                cols = pl.ds(pl.multiple_of(c * tile, tile), tile)
+                w = jnp.concatenate(
+                    [
+                        gathered[pl.ds(pair * 2, 2), t, :, cols].reshape(head, tile)
+                        for t in range(tps)
+                    ],
+                    axis=0,
+                )
+                result = dot(left, w)
+                if n > 0:
+                    result = result + partial[:, cols]
+                if n < chips - 1:
+                    partial[:, cols] = result
+                else:
+                    out_ref[:, cols] = result.astype(BF16)
+                return carry
+
+            lax.fori_loop(0, tiles, project, 0)
+    else:
+
+        def wait_passed(i, carry):
+            wait_slab(chip_source(i) + sibling - me)
+            return carry
+
+        lax.fori_loop(0, chips, wait_passed, 0)
+
+        def project(c, carry):
+            cols = pl.ds(pl.multiple_of(c * tile, tile), tile)
+            result = jnp.zeros((out_rows, tile), F32)
+            for t in range(tps):
+                w = gathered[:, t, :, cols].reshape(pools * part, tile)
+                result = result + dot(attended[t], w)
+            out_ref[:, cols] = result.astype(BF16)
+            return carry
+
+        lax.fori_loop(0, tiles, project, 0)
 
     def wait_sends(i, carry):
         q = lax.rem(me + i, pools)
@@ -653,6 +685,7 @@
             pltpu.VMEM((seats * head, wide), F32),
             pltpu.VMEM((seats, wide), F32),
             pltpu.VMEM((seats, wide), F32),
+            pltpu.VMEM((rows, out_cols), F32),
             dma((pools,)),
             dma((pools,)),
             dma((pools,)),

time: 149 us -> 152 us (1.020); the launches traced: 149 us -> 150 us
  Pallas kernels: 144 us -> 146 us
where the time goes in v1:
time: 152 us; the launch traced here: 150 us
  Pallas kernels  146 us (96%)
  local copies, waits for them, and re-layouts  4.48 us (3%)
    pallas_call x1, Pallas kernels, local(): pl.pallas_call(functools.partial(kernel, pools, tps, seats, cap), out_sha...  144 us
    unnamed x1, local copies, waits for them, and re-layouts  3.16 us

profile of v1, /device:TPU:0, one launch (start us, length us, event | category | flops | bytes accessed | tf_op | source)
XLA Modules:
  0.0 150.2 jit_solution(12197387682688281883)
XLA Ops:
  0.0 1.3 copy.14.seat_ref
  1.3 1.9 %shard_map.127.meta_ref = s32[40,8]{1,0:T(8,128)} custom-call(s32[16,1]{1,0:T(8,128)} %copy.14.seat_ref, s32[1,16]{1,0:T(1,128)} %bitcast.2, s32[16,32]{1,0:T(8,128)} %map_ref.1), custom_call_target="tpu_custom_call" | custom-call | tf_op jit(solution)/shard_map/pallas_call | solution.py:649
  3.3 143.8 %shard_map.128 = bf16[512,2048]{1,0:T(8,128)(2,1)} custom-call(s32[40,8]{1,0:T(8,128)} %shard_map.127.meta_ref, bf16[512,512]{1,0:T(8,128)(2,1)} %tq_ref.1, bf16[512,128]{1,0:T(8,128)(2,1)} %tk_ref.1, bf16[512,128]{1,0:T(8,128)(2,1)} %tv_ref.1, f32[33,128]{1,0:T(8,128)} %constant.10.clone.cos_far, f32[33,128]{1,0:T(8,128)} %constant.11.clone.sin_far, ...), custom_call_target="tpu_custom_call" | custom-call | tf_op jit(solution)/shard_map/pallas_call | solution.py:668
  147.1 3.2 %copy.16 = bf16[512,2048]{1,0:T(8,128)(2,1)} copy(bf16[512,2048]{1,0:T(8,128)(2,1)} %shard_map.128) | data formatting | bytes 4194304

commit v2 on v1

--- a/solution.py
+++ b/solution.py
@@ -195,8 +195,20 @@
     def _():
         scatter_copy(me).start()
 
+    def send_to(i):
+        if chips != 4:
+            return lax.rem(me + i, pools)
+        x = lax.rem(lax.rem(chip, 2) + lax.rem(i, 2), 2)
+        y = lax.rem(chip // 2 + lax.rem(i, 4) // 2, 2)
+        return (y * 2 + x) * 2 + lax.rem(core + i // 4, 2)
+
+    def sent_from(i):
+        if chips != 4:
+            return lax.rem(me + pools - i, pools)
+        return send_to(i)
+
     def start_kv(i, carry):
-        q = lax.rem(me + i, pools)
+        q = send_to(i)
         for r in range(cap):
             slot = meta_ref[q, r]
             send_k[q, r] = pool_k[slot]
@@ -205,7 +217,8 @@
             copy.start()
         return carry
 
-    lax.fori_loop(1, pools, start_kv, 0)
+    in_flight = min(3, pools - 1)
+    lax.fori_loop(1, 1 + in_flight, start_kv, 0)
     for r in range(cap):
         slot = meta_ref[me, r]
         keys[me, r] = pool_k[slot]
@@ -380,14 +393,20 @@
             total[e : e + 1, :] = sums[e]
 
     def step(i, carry):
-        source = lax.rem(me + pools - i, pools)
+        source = sent_from(i)
 
         @pl.when(i > 0)
         def _():
             for copy in kv_arrival(source):
                 copy.wait_recv()
-
-        @pl.when(i == pools - 1)
+            for copy in kv_copies(send_to(i)):
+                copy.wait_send()
+
+        @pl.when((i > 0) & (i < pools - in_flight))
+        def _():
+            start_kv(i + in_flight, 0)
+
+        @pl.when(i == pools - 2)
         def _():
             start_gather()
 
@@ -515,8 +534,6 @@
 
     def wait_sends(i, carry):
         q = lax.rem(me + i, pools)
-        for copy in kv_copies(q):
-            copy.wait_send()
         scatter_copy(q).wait_send()
         return carry
 

time: 152 us -> 158 us (1.039)
  Pallas kernels: 146 us -> 153 us
    pallas_call x1, Pallas kernels: 144 us -> 151 us  [local(): pl.pallas_call(functools.partial(kernel, pools, tps, seats, cap), out_sha...]
where the time goes in v2:
time: 158 us
  Pallas kernels  153 us (97%)
  local copies, waits for them, and re-layouts  4.48 us (3%)
    pallas_call x1, Pallas kernels, local(): pl.pallas_call(functools.partial(kernel, pools, tps, seats, cap), out_sha...  151 us

profile of v2, /device:TPU:0, one launch (start us, length us, event | category | flops | bytes accessed | tf_op | source)
XLA Modules:
  0.0 157.6 jit_solution(9581754203070878739)
XLA Ops:
  0.0 1.3 copy.14.seat_ref
  1.3 1.9 %shard_map.127.meta_ref = s32[40,8]{1,0:T(8,128)} custom-call(s32[16,1]{1,0:T(8,128)} %copy.14.seat_ref, s32[1,16]{1,0:T(1,128)} %bitcast.2, s32[16,32]{1,0:T(8,128)} %map_ref.1), custom_call_target="tpu_custom_call" | custom-call | tf_op jit(solution)/shard_map/pallas_call | solution.py:666
  3.3 151.1 %shard_map.128 = bf16[512,2048]{1,0:T(8,128)(2,1)} custom-call(s32[40,8]{1,0:T(8,128)} %shard_map.127.meta_ref, bf16[512,512]{1,0:T(8,128)(2,1)} %tq_ref.1, bf16[512,128]{1,0:T(8,128)(2,1)} %tk_ref.1, bf16[512,128]{1,0:T(8,128)(2,1)} %tv_ref.1, f32[33,128]{1,0:T(8,128)} %constant.10.clone.cos_far, f32[33,128]{1,0:T(8,128)} %constant.11.clone.sin_far, ...), custom_call_target="tpu_custom_call" | custom-call | tf_op jit(solution)/shard_map/pallas_call | solution.py:685
  154.4 3.2 %copy.16 = bf16[512,2048]{1,0:T(8,128)(2,1)} copy(bf16[512,2048]{1,0:T(8,128)(2,1)} %shard_map.128) | data formatting | bytes 4194304

commit v3 on v0

--- a/solution.py
+++ b/solution.py
@@ -47,6 +47,7 @@
     acc,
     top,
     total,
+    partial,
     k_send,
     k_recv,
     v_send,
@@ -378,6 +379,16 @@
             top[e : e + 1, :] = tops[e]
             total[e : e + 1, :] = sums[e]
 
+    if relay:
+        first, second = relay_sends()
+        passes = [
+            [(1, next_x, 0, first), (2, next_y, 1, second)],
+            [(1, next_x, 1), (2, next_y, 0)],
+            [(3, across, 0), (3, across, 1)],
+        ]
+    else:
+        passes = []
+
     def step(i, carry):
         source = lax.rem(me + pools - i, pools)
 
@@ -386,9 +397,16 @@
             for copy in kv_arrival(source):
                 copy.wait_recv()
 
-        @pl.when(i == pools - 3)
+        @pl.when(i == pools // 2 - 1)
         def _():
             start_gather()
+
+        for n, items in enumerate(passes[:2]):
+
+            @pl.when(i == pools - 2 + n)
+            def _(items=items):
+                for item in items:
+                    pass_on(*item)
 
         attend(source)
         return carry
@@ -432,24 +450,8 @@
             slot_copy(row + hop, row + 1, 1, 0).wait_recv()
 
     hop_sends(0, lambda copy: copy.start())
-    if relay:
-        first, second = relay_sends()
-        passes = [
-            [(1, next_x, 0, first), (2, next_y, 1, second)],
-            [(1, next_x, 1), (2, next_y, 0)],
-            [(3, across, 0), (3, across, 1)],
-        ]
-    else:
-        passes = []
-    for hop in range(1, tps):
-        if passes:
-            for item in passes.pop(0):
-                pass_on(*item)
-        hop_waits(hop)
-        if hop < tps - 1:
-            hop_sends(hop, lambda copy: copy.start())
-    for group_of in passes:
-        for item in group_of:
+    for items in passes[2:]:
+        for item in items:
             pass_on(*item)
     if not relay:
 
@@ -468,18 +470,36 @@
 
     lax.fori_loop(0, chips, wait_passed, 0)
 
-    tile = 256
-
-    def project(n, carry):
-        cols = pl.ds(pl.multiple_of(n * tile, tile), tile)
-        result = jnp.zeros((out_ref.shape[0], tile), F32)
-        for t in range(tps):
-            w = gathered[:, t, :, cols].reshape(pools * part, tile)
-            result = result + dot(attended[t], w)
-        out_ref[:, cols] = result.astype(BF16)
-        return carry
-
-    lax.fori_loop(0, out_ref.shape[1] // tile, project, 0)
+    tile = 512
+    tiles = out_ref.shape[1] // tile
+
+    def project(slot, first):
+        def one(c, carry):
+            cols = pl.ds(pl.multiple_of(c * tile, tile), tile)
+            w = gathered[:, slot, :, cols].reshape(pools * part, tile)
+            result = dot(attended[slot], w)
+            if not first:
+                result = result + partial[:, cols]
+            partial[:, cols] = result
+            return carry
+
+        lax.fori_loop(0, tiles, one, 0)
+
+    project(row, True)
+    for hop in range(1, tps):
+        hop_waits(hop)
+        if hop < tps - 1:
+            hop_sends(hop, lambda copy: copy.start())
+
+        @pl.when(row - hop >= 0)
+        def _():
+            project(row - hop, False)
+
+        @pl.when(row + hop < tps)
+        def _():
+            project(row + hop, False)
+
+    out_ref[...] = partial[...].astype(BF16)
 
     def wait_sends(i, carry):
         q = lax.rem(me + i, pools)
@@ -653,6 +673,7 @@
             pltpu.VMEM((seats * head, wide), F32),
             pltpu.VMEM((seats, wide), F32),
             pltpu.VMEM((seats, wide), F32),
+            pltpu.VMEM((rows, out_cols), F32),
             dma((pools,)),
             dma((pools,)),
             dma((pools,)),

time: 149 us -> 172 us (1.15)
  Pallas kernels: 144 us -> 167 us
    pallas_call x1, Pallas kernels: 143 us -> 165 us  [local(): pl.pallas_call(functools.partial(kernel, pools, tps, seats, cap), out_sha...]
where the time goes in v3:
time: 172 us; the launch traced here: 171 us
  Pallas kernels  167 us (97%)
  local copies, waits for them, and re-layouts  4.48 us (3%)
    pallas_call x1, Pallas kernels, local(): pl.pallas_call(functools.partial(kernel, pools, tps, seats, cap), out_sha...  165 us

profile of v3, /device:TPU:0, one launch (start us, length us, event | category | flops | bytes accessed | tf_op | source)
XLA Modules:
  0.0 171.4 jit_solution(13538364026718425415)
XLA Ops:
  0.0 1.3 copy.14.seat_ref
  1.3 1.9 %shard_map.127.meta_ref = s32[40,8]{1,0:T(8,128)} custom-call(s32[16,1]{1,0:T(8,128)} %copy.14.seat_ref, s32[1,16]{1,0:T(1,128)} %bitcast.2, s32[16,32]{1,0:T(8,128)} %map_ref.1), custom_call_target="tpu_custom_call" | custom-call | tf_op jit(solution)/shard_map/pallas_call | solution.py:637
  3.3 165.0 %shard_map.128 = bf16[512,2048]{1,0:T(8,128)(2,1)} custom-call(s32[40,8]{1,0:T(8,128)} %shard_map.127.meta_ref, bf16[512,512]{1,0:T(8,128)(2,1)} %tq_ref.1, bf16[512,128]{1,0:T(8,128)(2,1)} %tk_ref.1, bf16[512,128]{1,0:T(8,128)(2,1)} %tv_ref.1, f32[33,128]{1,0:T(8,128)} %constant.10.clone.cos_far, f32[33,128]{1,0:T(8,128)} %constant.11.clone.sin_far, ...), custom_call_target="tpu_custom_call" | custom-call | tf_op jit(solution)/shard_map/pallas_call | solution.py:656
  168.3 3.2 %copy.16 = bf16[512,2048]{1,0:T(8,128)(2,1)} copy(bf16[512,2048]{1,0:T(8,128)(2,1)} %shard_map.128) | data formatting | bytes 4194304
